TPU v7x, 32 devices: a whole 2x2x4 slice. The times are simulated.
32 devices in a mesh: gz: 4 (over y, x), gx: 8 (over z, core).
Axes of the slice: x: 2, y: 2, z: 4, core: 2. Of those that a mesh axis runs over, the one named last changes fastest.
Arguments:
- adj_fields: float32 [6, 128, 128, 8, 128], P(None, 'gx', 'gz'), may hold values from -6 to 6
- coef_e: float32 [128, 128, 8, 128], P('gx', 'gz'), may hold values from 0.1 to 0.6
- plane_z: int32 [2], replicated, may hold values from 0 to 127
- snap_index: int32 [1], replicated, may hold values from 0 to 2
- fwd_snaps: float32 [4, 2, 3, 128, 1024], P(None, None, None, 'gx', 'gz'), may hold values from -6 to 6
- design: float32 [2, 128, 1024], P(None, 'gx', 'gz'), may hold values from 0 to 1
- sens_in: float32 [2, 128, 1024], P(None, 'gx', 'gz'), may hold values from -6 to 6
Outputs:
- new_fields: float32 [6, 128, 128, 8, 128], P(None, 'gx', 'gz')
- gradient: float32 [2, 128, 1024], P(None, 'gx', 'gz')
Inputs may be any that keep to these rules, and one draw needn't show every extreme that they name: `plane_z`: the two design planes may lie in the same or in different z slabs.
All inputs are finite; a program needn't handle non-finite values.
Results may differ from a plain program's by a relative error of at most 0.00016.
Values sent between devices are 32-bit elements; how exact they have to be, the bound alone decides.
A program may use at most 128 MiB of HBM per device.

v0:
```python
import functools
import math

import jax
import jax.numpy as jnp
from jax import lax
from jax.experimental import pallas as pl
from jax.experimental.pallas import tpu as pltpu
from jax.sharding import PartitionSpec as P

R = 8
STEPS = 2
PLANES = 2
COMPS = 3
IMAGES = STEPS * PLANES * COMPS + 2 * PLANES
DESIGN = STEPS * PLANES * COMPS
SENS = DESIGN + PLANES
LANES = 128
SUBS = 8

magnetic_step = 0.5
sharpness = 8.0
threshold = 0.5

MESH = pl.DeviceIdType.MESH


def cone_table(radius):
    raw = [
        [max(0.0, radius - math.sqrt(a * a + b * b)) for b in range(radius + 1)]
        for a in range(radius + 1)
    ]
    total = sum(
        raw[abs(a)][abs(b)]
        for a in range(-radius, radius + 1)
        for b in range(-radius, radius + 1)
    )
    return [[entry / total for entry in line] for line in raw]


def projection_slope(filtered):
    scale_down = math.tanh(sharpness * threshold) + math.tanh(sharpness * (1.0 - threshold))
    return sharpness * (1.0 - jnp.tanh(sharpness * (filtered - threshold)) ** 2) / scale_down


def iota(shape, dim):
    return lax.broadcasted_iota(jnp.int32, shape, dim)


def ahead_y(v):
    n = v.ndim
    turned = pltpu.roll(v, LANES - 1, n - 1)
    carried = pltpu.roll(turned, SUBS - 1, n - 2)
    carried = jnp.where(iota(v.shape, n - 2) == SUBS - 1, 0.0, carried)
    return jnp.where(iota(v.shape, n - 1) == LANES - 1, carried, turned)


def behind_y(v):
    n = v.ndim
    turned = pltpu.roll(v, 1, n - 1)
    carried = pltpu.roll(turned, 1, n - 2)
    carried = jnp.where(iota(v.shape, n - 2) == 0, 0.0, carried)
    return jnp.where(iota(v.shape, n - 1) == 0, carried, turned)


def cone(ref, rows):
    table = cone_table(R)
    sums = [ref[:, :, R : R + rows]]
    for a in range(1, R):
        sums.append(ref[:, :, R - a : R - a + rows] + ref[:, :, R + a : R + a + rows])
    blocks = ref.shape[0]
    out = None
    for b in range(R):
        total = None
        for a in range(R):
            if table[a][b] > 0.0:
                term = table[a][b] * sums[a]
                total = term if total is None else total + term
        mid = total[1 : blocks - 1]
        if b == 0:
            out = mid
            continue
        lane = iota(mid.shape, 3)
        upper = jnp.where(lane < b, total[2:], mid)
        lower = jnp.where(lane >= LANES - b, total[: blocks - 2], mid)
        out = out + pltpu.roll(upper, LANES - b, 3) + pltpu.roll(lower, b, 3)
    return out


def kernel(
    gxn,
    gzn,
    fields,
    coef,
    plane_z,
    snap_index,
    fwd,
    design,
    sens_in,
    out,
    gradient,
    E,
    H,
    C,
    exr,
    ezr,
    gxr,
    gzr,
    cxr,
    czr,
    gxs,
    gzs,
    AG,
    DF,
    L,
    PT,
    RC,
    WV,
    step_send,
    step_recv,
    ag_send,
    ag_recv,
    rc_send,
    rc_recv,
    row_send,
    row_recv,
    load_sem,
    store_sem,
):
    X, Z = coef.shape[0], coef.shape[1]
    NB = coef.shape[2]
    TB = NB // gzn
    WB = TB + 2
    gx, gz = lax.axis_index("gx"), lax.axis_index("gz")
    has_xm, has_xp = gx > 0, gx < gxn - 1
    has_zm, has_zp = gz > 0, gz < gzn - 1

    def load(index, src, dst):
        return pltpu.make_async_copy(src, dst, load_sem.at[index])

    half = X // 2
    loads = [
        load(0, fields.at[0:3, X - 1], E.at[:, X - 1, 0:Z]),
        load(1, fields.at[3:6, X - 1], H.at[:, X, 1 : Z + 1]),
        load(2, fields.at[0:3, 0 : X - 1, Z - 1], E.at[:, 0 : X - 1, Z - 1]),
        load(3, fields.at[3:6, 0 : X - 1, Z - 1], H.at[:, 1:X, Z]),
        load(4, fields.at[0:3, 0:half, 0 : Z - 1], E.at[:, 0:half, 0 : Z - 1]),
        load(5, fields.at[3:6, 0:half, 0 : Z - 1], H.at[:, 1 : half + 1, 1:Z]),
        load(6, fields.at[0:3, half : X - 1, 0 : Z - 1], E.at[:, half : X - 1, 0 : Z - 1]),
        load(7, fields.at[3:6, half : X - 1, 0 : Z - 1], H.at[:, half + 1 : X, 1:Z]),
        load(8, coef, C),
    ]
    for copy in loads:
        copy.start()

    barrier = pltpu.get_barrier_semaphore()

    def greet(x, z):
        pl.semaphore_signal(barrier, inc=1, device_id={"gx": x, "gz": z}, device_id_type=MESH)

    for condition, x, z in (
        (has_xm, gx - 1, gz),
        (has_xp, gx + 1, gz),
        (has_xp & has_zm, gx + 1, gz - 1),
        (has_xm & has_zp, gx - 1, gz + 1),
    ):
        pl.when(condition)(functools.partial(greet, x, z))
    for d in range(1, gzn):
        greet(gx, lax.rem(gz + d, gzn))

    snap = snap_index[0]
    for block in range(TB):
        lanes = slice(block * LANES, (block + 1) * LANES)
        place = 2 + gz * TB + block
        for step in range(STEPS):
            for p in range(PLANES):
                for c in range(COMPS):
                    AG[place, (step * PLANES + p) * COMPS + c] = fwd[snap + step, p, c, :, lanes]
        AG[place, DESIGN:SENS] = design[:, :, lanes]
        AG[place, SENS:] = sens_in[:, :, lanes]
    pads = jnp.zeros((2, 2 * PLANES, X, LANES), jnp.float32)
    AG[0:2, DESIGN:] = pads
    AG[NB + 2 :, DESIGN:] = pads
    PT[0] = jnp.zeros(PT.shape[1:], jnp.float32)
    PT[NB + 1] = jnp.zeros(PT.shape[1:], jnp.float32)
    DF[:, :, 0:R] = jnp.zeros((TB + 4, PLANES, R, LANES), jnp.float32)
    DF[:, :, R + X :] = jnp.zeros((TB + 4, PLANES, R, LANES), jnp.float32)

    E[:, X] = jnp.zeros((COMPS, Z + 1, SUBS, LANES), jnp.float32)
    E[:, 0:X, Z] = jnp.zeros((COMPS, X, SUBS, LANES), jnp.float32)
    H[:, 0] = jnp.zeros((COMPS, Z + 1, SUBS, LANES), jnp.float32)
    H[:, 1:, 0] = jnp.zeros((COMPS, X, SUBS, LANES), jnp.float32)

    met = (
        has_xm.astype(jnp.int32)
        + has_xp.astype(jnp.int32)
        + (has_xp & has_zm).astype(jnp.int32)
        + (has_xm & has_zp).astype(jnp.int32)
        + (gzn - 1)
    )
    pl.semaphore_wait(barrier, met)

    def remote(src, dst, send, recv, x, z):
        return pltpu.make_async_remote_copy(
            src_ref=src,
            dst_ref=dst,
            send_sem=send,
            recv_sem=recv,
            device_id={"gx": x, "gz": z},
            device_id_type=MESH,
        )

    def step_copies(s):
        electric = fields if s == 0 else E

        def make(k, src, dst, x, z):
            return remote(src, dst, step_send.at[s, k], step_recv.at[s, k], x, z)

        return dict(
            ex=(make(0, electric.at[1:3, 0, 0:Z], exr.at[s], gx - 1, gz), has_xm, has_xp),
            ez=(make(1, electric.at[0:2, 0:X, 0], ezr.at[s], gx, gz - 1), has_zm, has_zp),
            cx=(
                make(2, electric.at[0, X - 1, 0], cxr.at[s], gx + 1, gz - 1),
                has_xp & has_zm,
                has_xm & has_zp,
            ),
            cz=(
                make(3, electric.at[2, 0, Z - 1], czr.at[s], gx - 1, gz + 1),
                has_xm & has_zp,
                has_xp & has_zm,
            ),
            gx=(make(4, gxs.at[s], gxr.at[s], gx + 1, gz), has_xp, has_xm),
            gz=(make(5, gzs.at[s], gzr.at[s], gx, gz + 1), has_zp, has_zm),
        )

    def start(item):
        pl.when(item[1])(item[0].start)

    def finish_send(item):
        pl.when(item[1])(item[0].wait_send)

    def fill_sends(s):
        E[0, X - 1, Z] = jnp.zeros((SUBS, LANES), jnp.float32)
        E[2, X, Z - 1] = jnp.zeros((SUBS, LANES), jnp.float32)
        ex, ey, ez = (E[c, X - 1, 0:Z] for c in range(3))
        gxs[s, 0] = H[1, X, 1:] + magnetic_step * (E[0, X - 1, 1 : Z + 1] - ex + ez)
        gxs[s, 1] = H[2, X, 1:] - magnetic_step * (ey + ahead_y(ex) - ex)
        ex, ey, ez = (E[c, 0:X, Z - 1] for c in range(3))
        gzs[s, 0] = H[0, 1:, Z] + magnetic_step * (ahead_y(ez) - ez + ey)
        gzs[s, 1] = H[1, 1:, Z] - magnetic_step * (ex + E[2, 1 : X + 1, Z - 1] - ez)

    def receive(s, copies):
        @pl.when(has_xp)
        def _():
            copies["ex"][0].wait_recv()
            E[1:3, X, 0:Z] = exr[s]

        @pl.when(has_zp)
        def _():
            copies["ez"][0].wait_recv()
            E[0:2, 0:X, Z] = ezr[s]

        @pl.when(has_xm)
        def _():
            copies["gx"][0].wait_recv()
            H[1, 0, 1:] = gxr[s, 0] - magnetic_step * E[2, 0, 0:Z]
            H[2, 0, 1:] = gxr[s, 1] + magnetic_step * E[1, 0, 0:Z]

        @pl.when(has_zm)
        def _():
            copies["gz"][0].wait_recv()
            H[0, 1:, 0] = gzr[s, 0] - magnetic_step * E[1, 0:X, 0]
            H[1, 1:, 0] = gzr[s, 1] + magnetic_step * E[0, 0:X, 0]

        @pl.when(has_xm & has_zp)
        def _():
            copies["cx"][0].wait_recv()
            H[1, 0, Z] = H[1, 0, Z] + magnetic_step * cxr[s]

        @pl.when(has_xp & has_zm)
        def _():
            copies["cz"][0].wait_recv()
            H[1, X, 0] = H[1, X, 0] - magnetic_step * czr[s]

    def update_h(x, z, n):
        here, next_z = pl.ds(z, n), pl.ds(z + 1, n)
        ex, ey, ez = (E[c, x, here] for c in range(3))
        ex_z, ey_z = E[0, x, next_z], E[1, x, next_z]
        ey_x, ez_x = E[1, x + 1, here], E[2, x + 1, here]
        H[0, x + 1, next_z] += magnetic_step * ((ahead_y(ez) - ez) - (ey_z - ey))
        H[1, x + 1, next_z] += magnetic_step * ((ex_z - ex) - (ez_x - ez))
        H[2, x + 1, next_z] += magnetic_step * ((ey_x - ey) - (ahead_y(ex) - ex))

    def new_e(x, z, n):
        before, here = pl.ds(z, n), pl.ds(z + 1, n)
        own = pl.ds(z, n)
        hx, hy, hz = (H[c, x + 1, here] for c in range(3))
        hx_z, hy_z = H[0, x + 1, before], H[1, x + 1, before]
        hy_x, hz_x = H[1, x, here], H[2, x, here]
        factor = C[x, own]
        return (
            E[0, x, own] - factor * ((hz - behind_y(hz)) - (hy - hy_z)),
            E[1, x, own] - factor * ((hx - hx_z) - (hz - hz_x)),
            E[2, x, own] - factor * ((hy - hy_x) - (hx - behind_y(hx))),
        )

    def chunks(stop, width=8):
        return [(z, min(width, stop - z)) for z in range(0, stop, width)]

    def sweep_h(x_stop, z_stop):
        @pl.loop(0, x_stop)
        def _(x):
            for z, n in chunks(z_stop):
                update_h(x, z, n)

    def sweep_e(x_start, x_stop):
        @pl.loop(x_start, x_stop)
        def _(x):
            for z, n in chunks(Z):
                E[0, x, z : z + n], E[1, x, z : z + n], E[2, x, z : z + n] = new_e(x, z, n)

    def layer_of(p):
        local = plane_z[p] - gz * Z
        inside = (local >= 0) & (local < Z)
        return jnp.clip(local, 0, Z - 1), jnp.where(inside, 1.0, 0.0).astype(jnp.float32)

    def products(step):
        @pl.loop(0, NB)
        def _(block):
            for p in range(PLANES):
                total = None
                for c in range(COMPS):
                    image = (step * PLANES + p) * COMPS + c
                    term = AG[block + 2, image] * L[step, p, c, :, block]
                    total = term if total is None else total + term
                if step:
                    total = PT[block + 1, p] + total
                PT[block + 1, p] = total

    copies = step_copies(0)
    for name in ("ex", "ez", "cx", "cz"):
        start(copies[name])
    for copy in loads[:4]:
        copy.wait()
    fill_sends(0)
    start(copies["gx"])
    start(copies["gz"])
    tile = pl.ds(2 + gz * TB, TB)
    gathers = [
        remote(AG.at[tile], AG.at[tile], ag_send.at[d], ag_recv.at[d], gx, lax.rem(gz + d, gzn))
        for d in range(1, gzn)
    ]
    for copy in gathers:
        copy.start()
    for copy in loads[4:]:
        copy.wait()
    receive(0, copies)
    sweep_h(X, Z)
    sweep_e(0, X)
    for item in copies.values():
        finish_send(item)

    copies = step_copies(1)
    for name in ("ex", "ez", "cx", "cz"):
        start(copies[name])
    fill_sends(1)
    start(copies["gx"])
    start(copies["gz"])
    sweep_h(X - 1, Z - 1)
    for p in range(PLANES):
        layer, inside = layer_of(p)
        for c in range(COMPS):
            L[0, p, c] = E[c, 0:X, layer] * inside
    for d in range(1, gzn):
        source = pl.ds(2 + lax.rem(gz + gzn - d, gzn) * TB, TB)
        remote(
            AG.at[tile], AG.at[source], ag_send.at[d], ag_recv.at[d], gx, lax.rem(gz + d, gzn)
        ).wait_recv()
    around = pl.ds(gz * TB, TB + 4)
    rows = [
        (
            remote(
                AG.at[around, DESIGN:SENS, X - R : X],
                DF.at[:, :, 0:R],
                row_send.at[0],
                row_recv.at[0],
                gx + 1,
                gz,
            ),
            has_xp,
            has_xm,
        ),
        (
            remote(
                AG.at[around, DESIGN:SENS, 0:R],
                DF.at[:, :, R + X : X + 2 * R],
                row_send.at[1],
                row_recv.at[1],
                gx - 1,
                gz,
            ),
            has_xm,
            has_xp,
        ),
    ]
    for item in rows:
        start(item)
    products(0)
    receive(1, copies)

    @pl.loop(0, X - 1)
    def _(x):
        update_h(x, Z - 1, 1)

    for z, n in chunks(Z):
        update_h(X - 1, z, n)
    for item in copies.values():
        finish_send(item)
    store_h = pltpu.make_async_copy(H.at[:, 1:, 1:], out.at[3:6], store_sem.at[0])
    store_h.start()

    for p in range(PLANES):
        layer, inside = layer_of(p)

        @pl.loop(0, X)
        def _(x):
            for c, value in enumerate(new_e(x, layer, 1)):
                L[1, p, c, x] = value[0] * inside

    products(1)
    partials = []
    for d in range(1, gzn):
        peer = lax.rem(gz + d, gzn)
        partials.append(
            remote(
                PT.at[pl.ds(peer * TB, WB)],
                RC.at[d],
                rc_send.at[d],
                rc_recv.at[d],
                gx,
                peer,
            )
        )
    for copy in partials:
        copy.start()
    sweep_e(0, half)
    store_low = pltpu.make_async_copy(
        E.at[:, 0:half, 0:Z], out.at[0:3, 0:half], store_sem.at[1]
    )
    store_low.start()
    sweep_e(half, X)
    store_high = pltpu.make_async_copy(
        E.at[:, half:X, 0:Z], out.at[0:3, half:X], store_sem.at[2]
    )
    store_high.start()

    DF[:, :, R : R + X] = AG[around, DESIGN:SENS]
    for item in rows:
        pl.when(item[2])(item[0].wait_recv)
    slope = projection_slope(cone(DF, X))
    total = AG[pl.ds(gz * TB + 1, WB), SENS:] + PT[pl.ds(gz * TB, WB)]
    for d, copy in enumerate(partials, 1):
        copy.wait_recv()
        total = total + RC[d]
    WV[:, :, R : R + X] = total * slope
    edges = [
        (
            remote(
                WV.at[:, :, X : X + R], WV.at[:, :, 0:R], row_send.at[2], row_recv.at[2], gx + 1, gz
            ),
            has_xp,
            has_xm,
        ),
        (
            remote(
                WV.at[:, :, R : 2 * R],
                WV.at[:, :, R + X : X + 2 * R],
                row_send.at[3],
                row_recv.at[3],
                gx - 1,
                gz,
            ),
            has_xm,
            has_xp,
        ),
    ]
    for item in edges:
        start(item)
    none = jnp.zeros((WB, PLANES, R, LANES), jnp.float32)

    @pl.when(gx == 0)
    def _():
        WV[:, :, 0:R] = none

    @pl.when(gx == gxn - 1)
    def _():
        WV[:, :, R + X :] = none

    for item in edges:
        pl.when(item[2])(item[0].wait_recv)
    result = cone(WV, X)
    for block in range(TB):
        gradient[:, :, block * LANES : (block + 1) * LANES] = result[block]

    for copy in gathers + partials:
        copy.wait_send()
    for item in rows + edges:
        finish_send(item)
    for copy in (store_h, store_low, store_high):
        copy.wait()


def shards(adj_fields, coef_e, plane_z, snap_index, fwd_snaps, design, sens_in):
    gxn, gzn = lax.axis_size("gx"), lax.axis_size("gz")
    X, Z, NB = coef_e.shape[0], coef_e.shape[1], coef_e.shape[2]
    TB = NB // gzn
    WB = TB + 2
    cell = (SUBS, LANES)

    def vmem(*shape):
        return pltpu.VMEM(shape, jnp.float32)

    hbm = pl.BlockSpec(memory_space=pl.ANY)
    smem = pl.BlockSpec(memory_space=pltpu.SMEM)
    local = pl.BlockSpec(memory_space=pltpu.VMEM)
    dma = pltpu.SemaphoreType.DMA
    return pl.pallas_call(
        functools.partial(kernel, gxn, gzn),
        out_shape=(
            jax.ShapeDtypeStruct(adj_fields.shape, jnp.float32),
            jax.ShapeDtypeStruct(design.shape, jnp.float32),
        ),
        in_specs=[hbm, hbm, smem, smem, local, local, local],
        out_specs=(hbm, local),
        scratch_shapes=[
            vmem(COMPS, X + 1, Z + 1, *cell),
            vmem(COMPS, X + 1, Z + 1, *cell),
            vmem(X, Z, *cell),
            vmem(STEPS, 2, Z, *cell),
            vmem(STEPS, 2, X, *cell),
            vmem(STEPS, 2, Z, *cell),
            vmem(STEPS, 2, X, *cell),
            vmem(STEPS, *cell),
            vmem(STEPS, *cell),
            vmem(STEPS, 2, Z, *cell),
            vmem(STEPS, 2, X, *cell),
            vmem(NB + 4, IMAGES, X, LANES),
            vmem(TB + 4, PLANES, X + 2 * R, LANES),
            vmem(STEPS, PLANES, COMPS, X, *cell),
            vmem(NB + 2, PLANES, X, LANES),
            vmem(gzn, WB, PLANES, X, LANES),
            vmem(WB, PLANES, X + 2 * R, LANES),
            dma((STEPS, 6)),
            dma((STEPS, 6)),
            dma((gzn,)),
            dma((gzn,)),
            dma((gzn,)),
            dma((gzn,)),
            dma((4,)),
            dma((4,)),
            dma((9,)),
            dma((3,)),
        ],
        compiler_params=pltpu.CompilerParams(
            collective_id=0, has_side_effects=True, vmem_limit_bytes=40 * 2**20
        ),
    )(adj_fields, coef_e, plane_z, snap_index, fwd_snaps, design, sens_in)


def solution(mesh):
    in_specs = (
        P(None, "gx", "gz", None, None),
        P("gx", "gz", None, None),
        P(),
        P(),
        P(None, None, None, "gx", "gz"),
        P(None, "gx", "gz"),
        P(None, "gx", "gz"),
    )
    out_specs = (P(None, "gx", "gz", None, None), P(None, "gx", "gz"))
    return jax.shard_map(shards, mesh=mesh, in_specs=in_specs, out_specs=out_specs, check_vma=False)
```

profile of v0, /device:TPU:1, one launch (start us, length us, event | category | flops | bytes accessed | tf_op | source)
XLA Modules:
  0.0 59.6 jit_solution(3945409877569232857)
XLA Ops:
  1.3 0.0 copy-start
  1.3 1.6 %copy-done = f32[16,32,8,128]{3,2,1,0:T(8,128)S(1)} copy-done((f32[16,32,8,128]{3,2,1,0:T(8,128)S(1)}, f32[16,32,8,128]{3,2,1,0:T(8,128)}, u32[]{:S(2)}) %copy-start) | copy-done | bytes 2097176
  2.9 0.0 copy-start.1
  2.9 1.0 %copy-done.1 = f32[4,2,3,16,256]{4,3,2,1,0:T(8,128)S(1)} copy-done((f32[4,2,3,16,256]{4,3,2,1,0:T(8,128)S(1)}, f32[4,2,3,16,256]{4,3,2,1,0:T(8,128)}, u32[]{:S(2)}) %copy-start.1) | copy-done | bytes 393240
  3.9 0.0 copy-start.2
  3.9 0.8 %copy-done.2 = f32[2,16,256]{2,1,0:T(8,128)S(1)} copy-done((f32[2,16,256]{2,1,0:T(8,128)S(1)}, f32[2,16,256]{2,1,0:T(8,128)}, u32[]{:S(2)}) %copy-start.2) | copy-done | bytes 32792
  4.6 0.0 copy-start.3
  4.6 0.8 %copy-done.3 = f32[2,16,256]{2,1,0:T(8,128)S(1)} copy-done((f32[2,16,256]{2,1,0:T(8,128)S(1)}, f32[2,16,256]{2,1,0:T(8,128)}, u32[]{:S(2)}) %copy-start.3) | copy-done | bytes 32792
  5.4 0.0 copy-start.4
  5.4 0.7 %copy-done.4 = s32[2]{0:T(128)S(1)} copy-done((s32[2]{0:T(128)S(1)}, s32[2]{0:T(128)}, u32[]{:S(2)}) %copy-start.4) | copy-done | bytes 32
  6.0 42.0 %shard_map.86 = (f32[6,16,32,8,128]{4,3,2,1,0:T(8,128)}, f32[2,16,256]{2,1,0:T(8,128)S(1)}) custom-call(f32[6,16,32,8,128]{4,3,2,1,0:T(8,128)} %fields.1, f32[16,32,8,128]{3,2,1,0:T(8,128)S(1)} %copy-done, s32[2]{0:T(128)S(1)} %copy-done.4, s32[1]{0:T(128)S(6)} %copy.11.snap_index, f32[4,2,3,16,256]{4,3,2,1,0:T(8,128)S(1)} %copy-done.1, ...), custom_call_target="tpu_custom_call" | custom-call | tf_op jit(solution)/shard_map/pallas_call | solution.py:527
  48.1 10.9 %copy.12 = f32[6,16,32,8,128]{4,3,2,1,0:T(8,128)} copy(f32[6,16,32,8,128]{4,3,2,1,0:T(8,128)} %get-tuple-element.4) | data formatting | bytes 25165824
  59.0 0.6 %copy.13 = f32[2,16,256]{2,1,0:T(8,128)} copy(f32[2,16,256]{2,1,0:T(8,128)S(1)} %get-tuple-element.5) | data formatting | bytes 65536
Async XLA Ops:
  1.3 1.6 %copy-start = (f32[16,32,8,128]{3,2,1,0:T(8,128)S(1)}, f32[16,32,8,128]{3,2,1,0:T(8,128)}, u32[]{:S(2)}) copy-start(f32[16,32,8,128]{3,2,1,0:T(8,128)} %coef.1) | copy-start | bytes 6291460
  2.9 1.0 %copy-start.1 = (f32[4,2,3,16,256]{4,3,2,1,0:T(8,128)S(1)}, f32[4,2,3,16,256]{4,3,2,1,0:T(8,128)}, u32[]{:S(2)}) copy-start(f32[4,2,3,16,256]{4,3,2,1,0:T(8,128)} %fwd.1) | copy-start | bytes 1179652
  3.9 0.8 %copy-start.2 = (f32[2,16,256]{2,1,0:T(8,128)S(1)}, f32[2,16,256]{2,1,0:T(8,128)}, u32[]{:S(2)}) copy-start(f32[2,16,256]{2,1,0:T(8,128)} %design.1) | copy-start | bytes 98308
  4.6 0.8 %copy-start.3 = (f32[2,16,256]{2,1,0:T(8,128)S(1)}, f32[2,16,256]{2,1,0:T(8,128)}, u32[]{:S(2)}) copy-start(f32[2,16,256]{2,1,0:T(8,128)} %sens_in.1) | copy-start | bytes 98308
  5.4 0.7 %copy-start.4 = (s32[2]{0:T(128)S(1)}, s32[2]{0:T(128)}, u32[]{:S(2)}) copy-start(s32[2]{0:T(128)} %plane_z.1) | copy-start | bytes 28
where the time goes:
time: 60 us; the launch traced here: 59.6 us
  Pallas kernels  42 us (70%)
  local copies, waits for them, and re-layouts  16.3 us (27%)
  between operations  1.3 us (2%)
    pallas_call x1, Pallas kernels, shards(): pl.pallas_call(functools.partial(kernel, gxn, gzn), out_shape=(jax.ShapeD...  42 us
    unnamed x12, local copies, waits for them, and re-layouts  16.3 us

commit v1 on v0

--- a/solution.py
+++ b/solution.py
@@ -94,11 +94,14 @@
     coef,
     plane_z,
     snap_index,
+    fwd_hbm,
+    design_hbm,
+    sens_hbm,
+    out,
+    gradient,
     fwd,
     design,
     sens_in,
-    out,
-    gradient,
     E,
     H,
     C,
@@ -113,6 +116,7 @@
     AG,
     DF,
     L,
+    SL,
     PT,
     RC,
     WV,
@@ -125,7 +129,6 @@
     row_send,
     row_recv,
     load_sem,
-    store_sem,
 ):
     X, Z = coef.shape[0], coef.shape[1]
     NB = coef.shape[2]
@@ -144,11 +147,14 @@
         load(1, fields.at[3:6, X - 1], H.at[:, X, 1 : Z + 1]),
         load(2, fields.at[0:3, 0 : X - 1, Z - 1], E.at[:, 0 : X - 1, Z - 1]),
         load(3, fields.at[3:6, 0 : X - 1, Z - 1], H.at[:, 1:X, Z]),
-        load(4, fields.at[0:3, 0:half, 0 : Z - 1], E.at[:, 0:half, 0 : Z - 1]),
-        load(5, fields.at[3:6, 0:half, 0 : Z - 1], H.at[:, 1 : half + 1, 1:Z]),
-        load(6, fields.at[0:3, half : X - 1, 0 : Z - 1], E.at[:, half : X - 1, 0 : Z - 1]),
-        load(7, fields.at[3:6, half : X - 1, 0 : Z - 1], H.at[:, half + 1 : X, 1:Z]),
-        load(8, coef, C),
+        load(4, fwd_hbm, fwd),
+        load(5, design_hbm, design),
+        load(6, sens_hbm, sens_in),
+        load(7, fields.at[0:3, 0 : X - 1, 0 : Z - 1], E.at[:, 0 : X - 1, 0 : Z - 1]),
+        load(8, fields.at[3:6, 0:half, 0 : Z - 1], H.at[:, 1 : half + 1, 1:Z]),
+        load(9, coef.at[0:half], C.at[0:half]),
+        load(10, fields.at[3:6, half : X - 1, 0 : Z - 1], H.at[:, half + 1 : X, 1:Z]),
+        load(11, coef.at[half:X], C.at[half:X]),
     ]
     for copy in loads:
         copy.start()
@@ -168,16 +174,6 @@
     for d in range(1, gzn):
         greet(gx, lax.rem(gz + d, gzn))
 
-    snap = snap_index[0]
-    for block in range(TB):
-        lanes = slice(block * LANES, (block + 1) * LANES)
-        place = 2 + gz * TB + block
-        for step in range(STEPS):
-            for p in range(PLANES):
-                for c in range(COMPS):
-                    AG[place, (step * PLANES + p) * COMPS + c] = fwd[snap + step, p, c, :, lanes]
-        AG[place, DESIGN:SENS] = design[:, :, lanes]
-        AG[place, SENS:] = sens_in[:, :, lanes]
     pads = jnp.zeros((2, 2 * PLANES, X, LANES), jnp.float32)
     AG[0:2, DESIGN:] = pads
     AG[NB + 2 :, DESIGN:] = pads
@@ -282,42 +278,46 @@
             copies["cz"][0].wait_recv()
             H[1, X, 0] = H[1, X, 0] - magnetic_step * czr[s]
 
-    def update_h(x, z, n):
-        here, next_z = pl.ds(z, n), pl.ds(z + 1, n)
-        ex, ey, ez = (E[c, x, here] for c in range(3))
-        ex_z, ey_z = E[0, x, next_z], E[1, x, next_z]
-        ey_x, ez_x = E[1, x + 1, here], E[2, x + 1, here]
-        H[0, x + 1, next_z] += magnetic_step * ((ahead_y(ez) - ez) - (ey_z - ey))
-        H[1, x + 1, next_z] += magnetic_step * ((ex_z - ex) - (ez_x - ez))
-        H[2, x + 1, next_z] += magnetic_step * ((ey_x - ey) - (ahead_y(ex) - ex))
-
-    def new_e(x, z, n):
-        before, here = pl.ds(z, n), pl.ds(z + 1, n)
-        own = pl.ds(z, n)
-        hx, hy, hz = (H[c, x + 1, here] for c in range(3))
-        hx_z, hy_z = H[0, x + 1, before], H[1, x + 1, before]
-        hy_x, hz_x = H[1, x, here], H[2, x, here]
-        factor = C[x, own]
+    def curl_h(e, next_x, next_z):
+        (ex, ey, ez), (ey_x, ez_x), (ex_z, ey_z) = e, next_x, next_z
         return (
-            E[0, x, own] - factor * ((hz - behind_y(hz)) - (hy - hy_z)),
-            E[1, x, own] - factor * ((hx - hx_z) - (hz - hz_x)),
-            E[2, x, own] - factor * ((hy - hy_x) - (hx - behind_y(hx))),
+            magnetic_step * ((ahead_y(ez) - ez) - (ey_z - ey)),
+            magnetic_step * ((ex_z - ex) - (ez_x - ez)),
+            magnetic_step * ((ey_x - ey) - (ahead_y(ex) - ex)),
         )
 
-    def chunks(stop, width=8):
-        return [(z, min(width, stop - z)) for z in range(0, stop, width)]
-
-    def sweep_h(x_stop, z_stop):
-        @pl.loop(0, x_stop)
-        def _(x):
-            for z, n in chunks(z_stop):
-                update_h(x, z, n)
-
-    def sweep_e(x_start, x_stop):
+    def new_e(e, h, before_x, before_z, factor):
+        (hx, hy, hz), (hy_x, hz_x), (hx_z, hy_z) = h, before_x, before_z
+        return (
+            e[0] - factor * ((hz - behind_y(hz)) - (hy - hy_z)),
+            e[1] - factor * ((hx - hx_z) - (hz - hz_x)),
+            e[2] - factor * ((hy - hy_x) - (hx - behind_y(hx))),
+        )
+
+    def sweep(s, x_start, x_stop, width=4):
         @pl.loop(x_start, x_stop)
         def _(x):
-            for z, n in chunks(Z):
-                E[0, x, z : z + n], E[1, x, z : z + n], E[2, x, z : z + n] = new_e(x, z, n)
+            below = (H[0, x + 1, 0:1], H[1, x + 1, 0:1])
+            for z in range(0, Z, width):
+                own, up = slice(z, z + width), slice(z + 1, z + width + 1)
+                ex, ey = E[0, x, z : z + width + 1], E[1, x, z : z + width + 1]
+                e = (ex[:-1], ey[:-1], E[2, x, own])
+                curl = curl_h(e, (E[1, x + 1, own], E[2, x + 1, own]), (ex[1:], ey[1:]))
+                h = tuple(H[c, x + 1, up] + curl[c] for c in range(COMPS))
+                before_z = tuple(
+                    jnp.concatenate([first, value[:-1]], axis=0) for first, value in zip(below, h)
+                )
+                below = (h[0][-1:], h[1][-1:])
+                e = new_e(e, h, (H[1, x, up], H[2, x, up]), before_z, C[x, own])
+                H[1, x + 1, up], H[2, x + 1, up] = h[1], h[2]
+                if s + 1 < STEPS:
+                    H[0, x + 1, up] = h[0]
+                    for c in range(COMPS):
+                        E[c, x, own] = e[c]
+                else:
+                    for c in range(COMPS):
+                        out[c, x, own] = e[c]
+                        out[COMPS + c, x, own] = h[c]
 
     def layer_of(p):
         local = plane_z[p] - gz * Z
@@ -337,6 +337,23 @@
                     total = PT[block + 1, p] + total
                 PT[block + 1, p] = total
 
+    def plane_e(layer):
+        def h_at(z):
+            e = tuple(E[c, 0:X, z] for c in range(COMPS))
+            curl = curl_h(
+                e, (E[1, 1 : X + 1, z], E[2, 1 : X + 1, z]), (E[0, 0:X, z + 1], E[1, 0:X, z + 1])
+            )
+            return e, tuple(H[c, 1 : X + 1, z + 1] + curl[c] for c in range(COMPS))
+
+        e, h = h_at(layer)
+        _, under = h_at(jnp.maximum(layer - 1, 0))
+        lowest = layer == 0
+        before_z = tuple(jnp.where(lowest, H[c, 1 : X + 1, 0], under[c]) for c in range(2))
+        before_x = tuple(
+            jnp.concatenate([H[c, 0:1, layer + 1], h[c][:-1]], axis=0) for c in (1, 2)
+        )
+        return new_e(e, h, before_x, before_z, C[0:X, layer])
+
     copies = step_copies(0)
     for name in ("ex", "ez", "cx", "cz"):
         start(copies[name])
@@ -345,6 +362,18 @@
     fill_sends(0)
     start(copies["gx"])
     start(copies["gz"])
+    for copy in loads[4:7]:
+        copy.wait()
+    snap = snap_index[0]
+    for block in range(TB):
+        lanes = slice(block * LANES, (block + 1) * LANES)
+        place = 2 + gz * TB + block
+        for step in range(STEPS):
+            for p in range(PLANES):
+                for c in range(COMPS):
+                    AG[place, (step * PLANES + p) * COMPS + c] = fwd[snap + step, p, c, :, lanes]
+        AG[place, DESIGN:SENS] = design[:, :, lanes]
+        AG[place, SENS:] = sens_in[:, :, lanes]
     tile = pl.ds(2 + gz * TB, TB)
     gathers = [
         remote(AG.at[tile], AG.at[tile], ag_send.at[d], ag_recv.at[d], gx, lax.rem(gz + d, gzn))
@@ -352,11 +381,13 @@
     ]
     for copy in gathers:
         copy.start()
-    for copy in loads[4:]:
+    for copy in loads[7:10]:
         copy.wait()
     receive(0, copies)
-    sweep_h(X, Z)
-    sweep_e(0, X)
+    sweep(0, 0, half)
+    for copy in loads[10:]:
+        copy.wait()
+    sweep(0, half, X)
     for item in copies.values():
         finish_send(item)
 
@@ -366,7 +397,6 @@
     fill_sends(1)
     start(copies["gx"])
     start(copies["gz"])
-    sweep_h(X - 1, Z - 1)
     for p in range(PLANES):
         layer, inside = layer_of(p)
         for c in range(COMPS):
@@ -406,27 +436,17 @@
     for item in rows:
         start(item)
     products(0)
+
+    DF[:, :, R : R + X] = AG[around, DESIGN:SENS]
+    for item in rows:
+        pl.when(item[2])(item[0].wait_recv)
+    SL[...] = projection_slope(cone(DF, X))
     receive(1, copies)
-
-    @pl.loop(0, X - 1)
-    def _(x):
-        update_h(x, Z - 1, 1)
-
-    for z, n in chunks(Z):
-        update_h(X - 1, z, n)
-    for item in copies.values():
-        finish_send(item)
-    store_h = pltpu.make_async_copy(H.at[:, 1:, 1:], out.at[3:6], store_sem.at[0])
-    store_h.start()
 
     for p in range(PLANES):
         layer, inside = layer_of(p)
-
-        @pl.loop(0, X)
-        def _(x):
-            for c, value in enumerate(new_e(x, layer, 1)):
-                L[1, p, c, x] = value[0] * inside
-
+        for c, value in enumerate(plane_e(layer)):
+            L[1, p, c] = value * inside
     products(1)
     partials = []
     for d in range(1, gzn):
@@ -443,26 +463,12 @@
         )
     for copy in partials:
         copy.start()
-    sweep_e(0, half)
-    store_low = pltpu.make_async_copy(
-        E.at[:, 0:half, 0:Z], out.at[0:3, 0:half], store_sem.at[1]
-    )
-    store_low.start()
-    sweep_e(half, X)
-    store_high = pltpu.make_async_copy(
-        E.at[:, half:X, 0:Z], out.at[0:3, half:X], store_sem.at[2]
-    )
-    store_high.start()
-
-    DF[:, :, R : R + X] = AG[around, DESIGN:SENS]
-    for item in rows:
-        pl.when(item[2])(item[0].wait_recv)
-    slope = projection_slope(cone(DF, X))
+    sweep(1, 0, X)
     total = AG[pl.ds(gz * TB + 1, WB), SENS:] + PT[pl.ds(gz * TB, WB)]
     for d, copy in enumerate(partials, 1):
         copy.wait_recv()
         total = total + RC[d]
-    WV[:, :, R : R + X] = total * slope
+    WV[:, :, R : R + X] = total * SL[...]
     edges = [
         (
             remote(
@@ -504,10 +510,8 @@
 
     for copy in gathers + partials:
         copy.wait_send()
-    for item in rows + edges:
+    for item in rows + edges + list(copies.values()):
         finish_send(item)
-    for copy in (store_h, store_low, store_high):
-        copy.wait()
 
 
 def shards(adj_fields, coef_e, plane_z, snap_index, fwd_snaps, design, sens_in):
@@ -520,19 +524,22 @@
     def vmem(*shape):
         return pltpu.VMEM(shape, jnp.float32)
 
-    hbm = pl.BlockSpec(memory_space=pl.ANY)
+    hbm = pl.BlockSpec(memory_space=pltpu.HBM)
     smem = pl.BlockSpec(memory_space=pltpu.SMEM)
     local = pl.BlockSpec(memory_space=pltpu.VMEM)
     dma = pltpu.SemaphoreType.DMA
     return pl.pallas_call(
         functools.partial(kernel, gxn, gzn),
         out_shape=(
-            jax.ShapeDtypeStruct(adj_fields.shape, jnp.float32),
-            jax.ShapeDtypeStruct(design.shape, jnp.float32),
+            pltpu.VMEM(adj_fields.shape, jnp.float32),
+            pltpu.VMEM(design.shape, jnp.float32),
         ),
-        in_specs=[hbm, hbm, smem, smem, local, local, local],
-        out_specs=(hbm, local),
+        in_specs=[hbm, hbm, smem, smem, hbm, hbm, hbm],
+        out_specs=(local, local),
         scratch_shapes=[
+            vmem(*fwd_snaps.shape),
+            vmem(*design.shape),
+            vmem(*sens_in.shape),
             vmem(COMPS, X + 1, Z + 1, *cell),
             vmem(COMPS, X + 1, Z + 1, *cell),
             vmem(X, Z, *cell),
@@ -547,6 +554,7 @@
             vmem(NB + 4, IMAGES, X, LANES),
             vmem(TB + 4, PLANES, X + 2 * R, LANES),
             vmem(STEPS, PLANES, COMPS, X, *cell),
+            vmem(WB, PLANES, X, LANES),
             vmem(NB + 2, PLANES, X, LANES),
             vmem(gzn, WB, PLANES, X, LANES),
             vmem(WB, PLANES, X + 2 * R, LANES),
@@ -558,11 +566,10 @@
             dma((gzn,)),
             dma((4,)),
             dma((4,)),
-            dma((9,)),
-            dma((3,)),
+            dma((12,)),
         ],
         compiler_params=pltpu.CompilerParams(
-            collective_id=0, has_side_effects=True, vmem_limit_bytes=40 * 2**20
+            collective_id=0, has_side_effects=True, vmem_limit_bytes=51 * 2**20
         ),
     )(adj_fields, coef_e, plane_z, snap_index, fwd_snaps, design, sens_in)
 

time: 60 us -> 45.4 us (0.76)
  local copies, waits for them, and re-layouts: 16.3 us -> 5.39 us
  Pallas kernels: 42 us -> 38.6 us
    unnamed x12 -> x2, local copies, waits for them, and re-layouts: 16.3 us -> 5.39 us
    pallas_call x1, Pallas kernels: 42 us -> 38.6 us  [shards(): pl.pallas_call(functools.partial(kernel, gxn, gzn), out_shape=(pltpu.VMEM...]
where the time goes in v1:
time: 45.4 us; the launch traced here: 45.3 us
  Pallas kernels  38.6 us (85%)
  local copies, waits for them, and re-layouts  5.39 us (12%)
  between operations  1.29 us (3%)
    pallas_call x1, Pallas kernels, shards(): pl.pallas_call(functools.partial(kernel, gxn, gzn), out_shape=(pltpu.VMEM...  38.6 us
    unnamed x2, local copies, waits for them, and re-layouts  5.39 us

profile of v1, /device:TPU:1, one launch (start us, length us, event | category | flops | bytes accessed | tf_op | source)
XLA Modules:
  0.0 45.3 jit_solution(2273272560635143864)
XLA Ops:
  1.3 38.6 %shard_map.86 = (f32[6,16,32,8,128]{4,3,2,1,0:T(8,128)S(1)}, f32[2,16,256]{2,1,0:T(8,128)S(1)}) custom-call(f32[6,16,32,8,128]{4,3,2,1,0:T(8,128)} %fields.1, f32[16,32,8,128]{3,2,1,0:T(8,128)} %coef.1, s32[2]{0:T(128)} %plane_z.1, s32[1]{0:T(128)S(6)} %copy.13.snap_index, f32[4,2,3,16,256]{4,3,2,1,0:T(8,128)} %fwd_hbm.1, f32[2,16,256]{2,1,0:T(8,128)} %design_hbm.1, ...), custom_call_target="tpu_custom_call" | custom-call | tf_op jit(solution)/shard_map/pallas_call | solution.py:531
  39.9 4.8 %copy.11 = f32[6,16,32,8,128]{4,3,2,1,0:T(8,128)} copy(f32[6,16,32,8,128]{4,3,2,1,0:T(8,128)S(1)} %get-tuple-element.2) | data formatting | bytes 25165824
  44.7 0.6 %copy.12 = f32[2,16,256]{2,1,0:T(8,128)} copy(f32[2,16,256]{2,1,0:T(8,128)S(1)} %get-tuple-element.3) | data formatting | bytes 65536

commit v2 on v1

--- a/solution.py
+++ b/solution.py
@@ -12,9 +12,6 @@
 STEPS = 2
 PLANES = 2
 COMPS = 3
-IMAGES = STEPS * PLANES * COMPS + 2 * PLANES
-DESIGN = STEPS * PLANES * COMPS
-SENS = DESIGN + PLANES
 LANES = 128
 SUBS = 8
 
@@ -100,7 +97,6 @@
     out,
     gradient,
     fwd,
-    design,
     sens_in,
     E,
     H,
@@ -113,30 +109,29 @@
     czr,
     gxs,
     gzs,
-    AG,
     DF,
     L,
+    LB,
+    LR,
     SL,
-    PT,
-    RC,
     WV,
     step_send,
     step_recv,
-    ag_send,
-    ag_recv,
-    rc_send,
-    rc_recv,
-    row_send,
-    row_recv,
+    layer_send,
+    layer_recv,
+    tile_send,
+    tile_recv,
     load_sem,
 ):
     X, Z = coef.shape[0], coef.shape[1]
     NB = coef.shape[2]
     TB = NB // gzn
-    WB = TB + 2
     gx, gz = lax.axis_index("gx"), lax.axis_index("gz")
     has_xm, has_xp = gx > 0, gx < gxn - 1
     has_zm, has_zp = gz > 0, gz < gzn - 1
+
+    DF[...] = jnp.zeros(DF.shape, jnp.float32)
+    WV[...] = jnp.zeros(WV.shape, jnp.float32)
 
     def load(index, src, dst):
         return pltpu.make_async_copy(src, dst, load_sem.at[index])
@@ -147,16 +142,23 @@
         load(1, fields.at[3:6, X - 1], H.at[:, X, 1 : Z + 1]),
         load(2, fields.at[0:3, 0 : X - 1, Z - 1], E.at[:, 0 : X - 1, Z - 1]),
         load(3, fields.at[3:6, 0 : X - 1, Z - 1], H.at[:, 1:X, Z]),
-        load(4, fwd_hbm, fwd),
-        load(5, design_hbm, design),
-        load(6, sens_hbm, sens_in),
-        load(7, fields.at[0:3, 0 : X - 1, 0 : Z - 1], E.at[:, 0 : X - 1, 0 : Z - 1]),
-        load(8, fields.at[3:6, 0:half, 0 : Z - 1], H.at[:, 1 : half + 1, 1:Z]),
-        load(9, coef.at[0:half], C.at[0:half]),
-        load(10, fields.at[3:6, half : X - 1, 0 : Z - 1], H.at[:, half + 1 : X, 1:Z]),
-        load(11, coef.at[half:X], C.at[half:X]),
+        load(4, fields.at[0:3, 0 : X - 1, 0 : Z - 1], E.at[:, 0 : X - 1, 0 : Z - 1]),
+        load(5, fields.at[3:6, 0:half, 0 : Z - 1], H.at[:, 1 : half + 1, 1:Z]),
+        load(6, coef.at[0:half], C.at[0:half]),
+        load(7, fields.at[3:6, half : X - 1, 0 : Z - 1], H.at[:, half + 1 : X, 1:Z]),
+        load(8, coef.at[half:X], C.at[half:X]),
+        load(9, fwd_hbm, fwd),
+        load(10, sens_hbm, sens_in),
     ]
-    for copy in loads:
+    designs = [
+        load(
+            11 + block,
+            design_hbm.at[:, :, block * LANES : (block + 1) * LANES],
+            DF.at[1 + block, :, R : R + X],
+        )
+        for block in range(TB)
+    ]
+    for copy in loads[:4] + designs + loads[4:]:
         copy.start()
 
     barrier = pltpu.get_barrier_semaphore()
@@ -169,18 +171,12 @@
         (has_xp, gx + 1, gz),
         (has_xp & has_zm, gx + 1, gz - 1),
         (has_xm & has_zp, gx - 1, gz + 1),
+        (has_xp & has_zp, gx + 1, gz + 1),
+        (has_xm & has_zm, gx - 1, gz - 1),
     ):
         pl.when(condition)(functools.partial(greet, x, z))
     for d in range(1, gzn):
         greet(gx, lax.rem(gz + d, gzn))
-
-    pads = jnp.zeros((2, 2 * PLANES, X, LANES), jnp.float32)
-    AG[0:2, DESIGN:] = pads
-    AG[NB + 2 :, DESIGN:] = pads
-    PT[0] = jnp.zeros(PT.shape[1:], jnp.float32)
-    PT[NB + 1] = jnp.zeros(PT.shape[1:], jnp.float32)
-    DF[:, :, 0:R] = jnp.zeros((TB + 4, PLANES, R, LANES), jnp.float32)
-    DF[:, :, R + X :] = jnp.zeros((TB + 4, PLANES, R, LANES), jnp.float32)
 
     E[:, X] = jnp.zeros((COMPS, Z + 1, SUBS, LANES), jnp.float32)
     E[:, 0:X, Z] = jnp.zeros((COMPS, X, SUBS, LANES), jnp.float32)
@@ -192,6 +188,8 @@
         + has_xp.astype(jnp.int32)
         + (has_xp & has_zm).astype(jnp.int32)
         + (has_xm & has_zp).astype(jnp.int32)
+        + (has_xp & has_zp).astype(jnp.int32)
+        + (has_xm & has_zm).astype(jnp.int32)
         + (gzn - 1)
     )
     pl.semaphore_wait(barrier, met)
@@ -228,6 +226,51 @@
             gx=(make(4, gxs.at[s], gxr.at[s], gx + 1, gz), has_xp, has_xm),
             gz=(make(5, gzs.at[s], gzr.at[s], gx, gz + 1), has_zp, has_zm),
         )
+
+    def tile_copies(first, ref):
+        has = {(-1, 0): has_xm, (1, 0): has_xp, (0, -1): has_zm, (0, 1): has_zp}
+        row_from = {0: slice(R, R + X), 1: slice(X, X + R), -1: slice(R, 2 * R)}
+        row_to = {0: slice(R, R + X), 1: slice(0, R), -1: slice(R + X, X + 2 * R)}
+        block_from = {0: slice(1, TB + 1), 1: slice(TB, TB + 1), -1: slice(1, 2)}
+        block_to = {0: slice(1, TB + 1), 1: slice(0, 1), -1: slice(TB + 1, TB + 2)}
+
+        def exists(dx, dz):
+            if not dz:
+                return has[dx, 0]
+            return has[0, dz] if not dx else has[dx, 0] & has[0, dz]
+
+        items = []
+        for dx in (0, 1, -1):
+            for dz in (0, 1, -1):
+                if not (dx or dz):
+                    continue
+                k = first + len(items)
+                copy = remote(
+                    ref.at[block_from[dz], :, row_from[dx]],
+                    ref.at[block_to[dz], :, row_to[dx]],
+                    tile_send.at[k],
+                    tile_recv.at[k],
+                    gx + dx,
+                    gz + dz,
+                )
+                items.append((copy, exists(dx, dz), exists(-dx, -dz)))
+        return items
+
+    def layer_copies(s):
+        copies = []
+        for d in range(1, gzn):
+            peer = lax.rem(gz + d, gzn)
+            copies.append(
+                remote(
+                    LB.at[s, pl.ds(peer * TB, TB)],
+                    LR.at[s, d],
+                    layer_send.at[s, d],
+                    layer_recv.at[s, d],
+                    gx,
+                    peer,
+                )
+            )
+        return copies
 
     def start(item):
         pl.when(item[1])(item[0].start)
@@ -324,18 +367,19 @@
         inside = (local >= 0) & (local < Z)
         return jnp.clip(local, 0, Z - 1), jnp.where(inside, 1.0, 0.0).astype(jnp.float32)
 
-    def products(step):
-        @pl.loop(0, NB)
-        def _(block):
+    def send_layers(s, new_layers):
+        for p in range(PLANES):
+            layer, inside = layer_of(p)
+            for c, value in enumerate(new_layers(layer)):
+                L[s, p, c] = value * inside
+        for block in range(NB):
             for p in range(PLANES):
-                total = None
                 for c in range(COMPS):
-                    image = (step * PLANES + p) * COMPS + c
-                    term = AG[block + 2, image] * L[step, p, c, :, block]
-                    total = term if total is None else total + term
-                if step:
-                    total = PT[block + 1, p] + total
-                PT[block + 1, p] = total
+                    LB[s, block, p * COMPS + c] = L[s, p, c, :, block]
+        copies = layer_copies(s)
+        for copy in copies:
+            copy.start()
+        return copies
 
     def plane_e(layer):
         def h_at(z):
@@ -362,30 +406,16 @@
     fill_sends(0)
     start(copies["gx"])
     start(copies["gz"])
+    for copy in designs:
+        copy.wait()
+    design_edges = tile_copies(0, DF)
+    for item in design_edges:
+        start(item)
     for copy in loads[4:7]:
-        copy.wait()
-    snap = snap_index[0]
-    for block in range(TB):
-        lanes = slice(block * LANES, (block + 1) * LANES)
-        place = 2 + gz * TB + block
-        for step in range(STEPS):
-            for p in range(PLANES):
-                for c in range(COMPS):
-                    AG[place, (step * PLANES + p) * COMPS + c] = fwd[snap + step, p, c, :, lanes]
-        AG[place, DESIGN:SENS] = design[:, :, lanes]
-        AG[place, SENS:] = sens_in[:, :, lanes]
-    tile = pl.ds(2 + gz * TB, TB)
-    gathers = [
-        remote(AG.at[tile], AG.at[tile], ag_send.at[d], ag_recv.at[d], gx, lax.rem(gz + d, gzn))
-        for d in range(1, gzn)
-    ]
-    for copy in gathers:
-        copy.start()
-    for copy in loads[7:10]:
         copy.wait()
     receive(0, copies)
     sweep(0, 0, half)
-    for copy in loads[10:]:
+    for copy in loads[7:]:
         copy.wait()
     sweep(0, half, X)
     for item in copies.values():
@@ -397,120 +427,41 @@
     fill_sends(1)
     start(copies["gx"])
     start(copies["gz"])
-    for p in range(PLANES):
-        layer, inside = layer_of(p)
-        for c in range(COMPS):
-            L[0, p, c] = E[c, 0:X, layer] * inside
-    for d in range(1, gzn):
-        source = pl.ds(2 + lax.rem(gz + gzn - d, gzn) * TB, TB)
-        remote(
-            AG.at[tile], AG.at[source], ag_send.at[d], ag_recv.at[d], gx, lax.rem(gz + d, gzn)
-        ).wait_recv()
-    around = pl.ds(gz * TB, TB + 4)
-    rows = [
-        (
-            remote(
-                AG.at[around, DESIGN:SENS, X - R : X],
-                DF.at[:, :, 0:R],
-                row_send.at[0],
-                row_recv.at[0],
-                gx + 1,
-                gz,
-            ),
-            has_xp,
-            has_xm,
-        ),
-        (
-            remote(
-                AG.at[around, DESIGN:SENS, 0:R],
-                DF.at[:, :, R + X : X + 2 * R],
-                row_send.at[1],
-                row_recv.at[1],
-                gx - 1,
-                gz,
-            ),
-            has_xm,
-            has_xp,
-        ),
-    ]
-    for item in rows:
-        start(item)
-    products(0)
-
-    DF[:, :, R : R + X] = AG[around, DESIGN:SENS]
-    for item in rows:
+    layers = send_layers(0, lambda z: tuple(E[c, 0:X, z] for c in range(COMPS)))
+
+    for item in design_edges:
         pl.when(item[2])(item[0].wait_recv)
     SL[...] = projection_slope(cone(DF, X))
     receive(1, copies)
 
-    for p in range(PLANES):
-        layer, inside = layer_of(p)
-        for c, value in enumerate(plane_e(layer)):
-            L[1, p, c] = value * inside
-    products(1)
-    partials = []
-    for d in range(1, gzn):
-        peer = lax.rem(gz + d, gzn)
-        partials.append(
-            remote(
-                PT.at[pl.ds(peer * TB, WB)],
-                RC.at[d],
-                rc_send.at[d],
-                rc_recv.at[d],
-                gx,
-                peer,
-            )
-        )
-    for copy in partials:
-        copy.start()
+    layers += send_layers(1, plane_e)
     sweep(1, 0, X)
-    total = AG[pl.ds(gz * TB + 1, WB), SENS:] + PT[pl.ds(gz * TB, WB)]
-    for d, copy in enumerate(partials, 1):
+
+    for copy in layers:
         copy.wait_recv()
-        total = total + RC[d]
-    WV[:, :, R : R + X] = total * SL[...]
-    edges = [
-        (
-            remote(
-                WV.at[:, :, X : X + R], WV.at[:, :, 0:R], row_send.at[2], row_recv.at[2], gx + 1, gz
-            ),
-            has_xp,
-            has_xm,
-        ),
-        (
-            remote(
-                WV.at[:, :, R : 2 * R],
-                WV.at[:, :, R + X : X + 2 * R],
-                row_send.at[3],
-                row_recv.at[3],
-                gx - 1,
-                gz,
-            ),
-            has_xm,
-            has_xp,
-        ),
-    ]
-    for item in edges:
+    snap = snap_index[0]
+    for block in range(TB):
+        lanes = slice(block * LANES, (block + 1) * LANES)
+        total = sens_in[:, :, lanes]
+        for step in range(STEPS):
+            electric = LB[step, gz * TB + block]
+            for d in range(1, gzn):
+                electric = electric + LR[step, d, block]
+            electric = electric.reshape(PLANES, COMPS, X, LANES)
+            total = total + jnp.sum(fwd[snap + step, :, :, :, lanes] * electric, axis=1)
+        WV[1 + block, :, R : R + X] = total * SL[block]
+    weighted_edges = tile_copies(8, WV)
+    for item in weighted_edges:
         start(item)
-    none = jnp.zeros((WB, PLANES, R, LANES), jnp.float32)
-
-    @pl.when(gx == 0)
-    def _():
-        WV[:, :, 0:R] = none
-
-    @pl.when(gx == gxn - 1)
-    def _():
-        WV[:, :, R + X :] = none
-
-    for item in edges:
+    for item in weighted_edges:
         pl.when(item[2])(item[0].wait_recv)
     result = cone(WV, X)
     for block in range(TB):
         gradient[:, :, block * LANES : (block + 1) * LANES] = result[block]
 
-    for copy in gathers + partials:
+    for copy in layers:
         copy.wait_send()
-    for item in rows + edges + list(copies.values()):
+    for item in design_edges + weighted_edges + list(copies.values()):
         finish_send(item)
 
 
@@ -518,7 +469,6 @@
     gxn, gzn = lax.axis_size("gx"), lax.axis_size("gz")
     X, Z, NB = coef_e.shape[0], coef_e.shape[1], coef_e.shape[2]
     TB = NB // gzn
-    WB = TB + 2
     cell = (SUBS, LANES)
 
     def vmem(*shape):
@@ -538,7 +488,6 @@
         out_specs=(local, local),
         scratch_shapes=[
             vmem(*fwd_snaps.shape),
-            vmem(*design.shape),
             vmem(*sens_in.shape),
             vmem(COMPS, X + 1, Z + 1, *cell),
             vmem(COMPS, X + 1, Z + 1, *cell),
@@ -551,22 +500,19 @@
             vmem(STEPS, *cell),
             vmem(STEPS, 2, Z, *cell),
             vmem(STEPS, 2, X, *cell),
-            vmem(NB + 4, IMAGES, X, LANES),
-            vmem(TB + 4, PLANES, X + 2 * R, LANES),
+            vmem(TB + 2, PLANES, X + 2 * R, LANES),
             vmem(STEPS, PLANES, COMPS, X, *cell),
-            vmem(WB, PLANES, X, LANES),
-            vmem(NB + 2, PLANES, X, LANES),
-            vmem(gzn, WB, PLANES, X, LANES),
-            vmem(WB, PLANES, X + 2 * R, LANES),
+            vmem(STEPS, NB, PLANES * COMPS, X, LANES),
+            vmem(STEPS, gzn, TB, PLANES * COMPS, X, LANES),
+            vmem(TB, PLANES, X, LANES),
+            vmem(TB + 2, PLANES, X + 2 * R, LANES),
             dma((STEPS, 6)),
             dma((STEPS, 6)),
-            dma((gzn,)),
-            dma((gzn,)),
-            dma((gzn,)),
-            dma((gzn,)),
-            dma((4,)),
-            dma((4,)),
-            dma((12,)),
+            dma((STEPS, gzn)),
+            dma((STEPS, gzn)),
+            dma((16,)),
+            dma((16,)),
+            dma((11 + TB,)),
         ],
         compiler_params=pltpu.CompilerParams(
             collective_id=0, has_side_effects=True, vmem_limit_bytes=51 * 2**20

time: 45.4 us -> 47.2 us (1.040)
  Pallas kernels: 38.6 us -> 40.4 us
    pallas_call x1, Pallas kernels: 38.6 us -> 40.4 us  [shards(): pl.pallas_call(functools.partial(kernel, gxn, gzn), out_shape=(pltpu.VMEM...]
where the time goes in v2:
time: 47.2 us; the launch traced here: 47 us
  Pallas kernels  40.4 us (86%)
  local copies, waits for them, and re-layouts  5.39 us (11%)
  between operations  1.29 us (3%)
    pallas_call x1, Pallas kernels, shards(): pl.pallas_call(functools.partial(kernel, gxn, gzn), out_shape=(pltpu.VMEM...  40.4 us
    unnamed x2, local copies, waits for them, and re-layouts  5.39 us

profile of v2, /device:TPU:1, one launch (start us, length us, event | category | flops | bytes accessed | tf_op | source)
XLA Modules:
  0.0 47.0 jit_solution(10732393077832504973)
XLA Ops:
  1.3 40.4 %shard_map.86 = (f32[6,16,32,8,128]{4,3,2,1,0:T(8,128)S(1)}, f32[2,16,256]{2,1,0:T(8,128)S(1)}) custom-call(f32[6,16,32,8,128]{4,3,2,1,0:T(8,128)} %fields.1, f32[16,32,8,128]{3,2,1,0:T(8,128)} %coef.1, s32[2]{0:T(128)} %plane_z.1, s32[1]{0:T(128)S(6)} %copy.13.snap_index, f32[4,2,3,16,256]{4,3,2,1,0:T(8,128)} %fwd_hbm.1, f32[2,16,256]{2,1,0:T(8,128)} %design_hbm.1, ...), custom_call_target="tpu_custom_call" | custom-call | tf_op jit(solution)/shard_map/pallas_call | solution.py:481
  41.6 4.8 %copy.11 = f32[6,16,32,8,128]{4,3,2,1,0:T(8,128)} copy(f32[6,16,32,8,128]{4,3,2,1,0:T(8,128)S(1)} %get-tuple-element.2) | data formatting | bytes 25165824
  46.4 0.6 %copy.12 = f32[2,16,256]{2,1,0:T(8,128)} copy(f32[2,16,256]{2,1,0:T(8,128)S(1)} %get-tuple-element.3) | data formatting | bytes 65536

commit v3 on v1

--- a/solution.py
+++ b/solution.py
@@ -105,6 +105,8 @@
     E,
     H,
     C,
+    EY,
+    HY,
     exr,
     ezr,
     gxr,
@@ -294,30 +296,65 @@
             e[2] - factor * ((hy - hy_x) - (hx - behind_y(hx))),
         )
 
-    def sweep(s, x_start, x_stop, width=4):
-        @pl.loop(x_start, x_stop)
+    CHUNKS = [(z, min(8, Z - z)) for z in range(0, Z, 8)]
+
+    def shift_e(x):
+        for z, n in CHUNKS:
+            EY[0, z : z + n] = ahead_y(E[0, x, z : z + n])
+            EY[1, z : z + n] = ahead_y(E[2, x, z : z + n])
+
+    def shift_h(x):
+        for z, n in CHUNKS:
+            HY[0, z : z + n] = behind_y(H[0, x + 1, z + 1 : z + n + 1])
+            HY[1, z : z + n] = behind_y(H[2, x + 1, z + 1 : z + n + 1])
+
+    def layer_h(s, x):
+        for z, n in CHUNKS:
+            own, up = slice(z, z + n), slice(z + 1, z + n + 1)
+            ex, ey, ez = (E[c, x, own] for c in range(COMPS))
+            h = (
+                H[0, x + 1, up] + magnetic_step * ((EY[1, own] - ez) - (E[1, x, up] - ey)),
+                H[1, x + 1, up]
+                + magnetic_step * ((E[0, x, up] - ex) - (E[2, x + 1, own] - ez)),
+                H[2, x + 1, up] + magnetic_step * ((E[1, x + 1, own] - ey) - (EY[0, own] - ex)),
+            )
+            for c in range(COMPS):
+                H[c, x + 1, up] = h[c]
+                if s + 1 == STEPS:
+                    out[COMPS + c, x, own] = h[c]
+
+    def layer_e(s, x):
+        for z, n in CHUNKS:
+            own, up = slice(z, z + n), slice(z + 1, z + n + 1)
+            hx, hy, hz = (H[c, x + 1, up] for c in range(COMPS))
+            factor = C[x, own]
+            e = (
+                E[0, x, own] - factor * ((hz - HY[1, own]) - (hy - H[1, x + 1, own])),
+                E[1, x, own] - factor * ((hx - H[0, x + 1, own]) - (hz - H[2, x, up])),
+                E[2, x, own] - factor * ((hy - H[1, x, up]) - (hx - HY[0, own])),
+            )
+            for c in range(COMPS):
+                if s + 1 == STEPS:
+                    out[c, x, own] = e[c]
+                else:
+                    E[c, x, own] = e[c]
+
+    def sweep(s, x_start, x_stop):
+        if x_start == 0:
+            shift_e(0)
+            layer_h(s, 0)
+            shift_e(1)
+            shift_h(0)
+
+        @pl.loop(max(x_start, 1), x_stop)
         def _(x):
-            below = (H[0, x + 1, 0:1], H[1, x + 1, 0:1])
-            for z in range(0, Z, width):
-                own, up = slice(z, z + width), slice(z + 1, z + width + 1)
-                ex, ey = E[0, x, z : z + width + 1], E[1, x, z : z + width + 1]
-                e = (ex[:-1], ey[:-1], E[2, x, own])
-                curl = curl_h(e, (E[1, x + 1, own], E[2, x + 1, own]), (ex[1:], ey[1:]))
-                h = tuple(H[c, x + 1, up] + curl[c] for c in range(COMPS))
-                before_z = tuple(
-                    jnp.concatenate([first, value[:-1]], axis=0) for first, value in zip(below, h)
-                )
-                below = (h[0][-1:], h[1][-1:])
-                e = new_e(e, h, (H[1, x, up], H[2, x, up]), before_z, C[x, own])
-                H[1, x + 1, up], H[2, x + 1, up] = h[1], h[2]
-                if s + 1 < STEPS:
-                    H[0, x + 1, up] = h[0]
-                    for c in range(COMPS):
-                        E[c, x, own] = e[c]
-                else:
-                    for c in range(COMPS):
-                        out[c, x, own] = e[c]
-                        out[COMPS + c, x, own] = h[c]
+            layer_h(s, x)
+            layer_e(s, x - 1)
+            shift_e(x + 1)
+            shift_h(x)
+
+        if x_stop == X:
+            layer_e(s, X - 1)
 
     def layer_of(p):
         local = plane_z[p] - gz * Z
@@ -543,6 +580,8 @@
             vmem(COMPS, X + 1, Z + 1, *cell),
             vmem(COMPS, X + 1, Z + 1, *cell),
             vmem(X, Z, *cell),
+            vmem(2, Z, *cell),
+            vmem(2, Z, *cell),
             vmem(STEPS, 2, Z, *cell),
             vmem(STEPS, 2, X, *cell),
             vmem(STEPS, 2, Z, *cell),

time: 45.4 us -> 45.4 us (level)
  no operation moved by 1% of the time
where the time goes in v3:
time: 45.4 us; the launch traced here: 45.3 us
  Pallas kernels  38.6 us (85%)
  local copies, waits for them, and re-layouts  5.39 us (12%)
  between operations  1.29 us (3%)
    pallas_call x1, Pallas kernels, shards(): pl.pallas_call(functools.partial(kernel, gxn, gzn), out_shape=(pltpu.VMEM...  38.6 us
    unnamed x2, local copies, waits for them, and re-layouts  5.39 us

profile of v3, /device:TPU:1, one launch (start us, length us, event | category | flops | bytes accessed | tf_op | source)
XLA Modules:
  0.0 45.3 jit_solution(12665215828054169843)
XLA Ops:
  1.3 38.6 %shard_map.86 = (f32[6,16,32,8,128]{4,3,2,1,0:T(8,128)S(1)}, f32[2,16,256]{2,1,0:T(8,128)S(1)}) custom-call(f32[6,16,32,8,128]{4,3,2,1,0:T(8,128)} %fields.1, f32[16,32,8,128]{3,2,1,0:T(8,128)} %coef.1, s32[2]{0:T(128)} %plane_z.1, s32[1]{0:T(128)S(6)} %copy.13.snap_index, f32[4,2,3,16,256]{4,3,2,1,0:T(8,128)} %fwd_hbm.1, f32[2,16,256]{2,1,0:T(8,128)} %design_hbm.1, ...), custom_call_target="tpu_custom_call" | custom-call | tf_op jit(solution)/shard_map/pallas_call | solution.py:568
  39.9 4.8 %copy.11 = f32[6,16,32,8,128]{4,3,2,1,0:T(8,128)} copy(f32[6,16,32,8,128]{4,3,2,1,0:T(8,128)S(1)} %get-tuple-element.2) | data formatting | bytes 25165824
  44.7 0.6 %copy.12 = f32[2,16,256]{2,1,0:T(8,128)} copy(f32[2,16,256]{2,1,0:T(8,128)S(1)} %get-tuple-element.3) | data formatting | bytes 65536

commit v4 on v3

--- a/solution.py
+++ b/solution.py
@@ -63,11 +63,31 @@
     return jnp.where(iota(v.shape, n - 1) == 0, carried, turned)
 
 
-def cone(ref, rows):
+def ahead_pair(a, b):
+    n = a.ndim
+    sub, lane = iota(a.shape, n - 2), iota(a.shape, n - 1)
+    turned = pltpu.roll(b, LANES - 1, n - 1)
+    carried = pltpu.roll(jnp.where(lane == 0, a, turned), SUBS - 1, n - 2)
+    carried = jnp.where(sub == SUBS - 1, 0.0, carried)
+    first = pltpu.roll(jnp.where(lane == 0, carried, a), LANES - 1, n - 1)
+    return first, jnp.where(lane == LANES - 1, carried, turned)
+
+
+def behind_pair(a, b):
+    n = a.ndim
+    sub, lane = iota(a.shape, n - 2), iota(a.shape, n - 1)
+    turned = pltpu.roll(b, 1, n - 1)
+    carried = pltpu.roll(jnp.where(lane == LANES - 1, a, turned), 1, n - 2)
+    carried = jnp.where(sub == 0, 0.0, carried)
+    first = pltpu.roll(jnp.where(lane == LANES - 1, carried, a), 1, n - 1)
+    return first, jnp.where(lane == 0, carried, turned)
+
+
+def cone(ref, p, rows):
     table = cone_table(R)
-    sums = [ref[:, :, R : R + rows]]
+    sums = [ref[:, p, R : R + rows]]
     for a in range(1, R):
-        sums.append(ref[:, :, R - a : R - a + rows] + ref[:, :, R + a : R + a + rows])
+        sums.append(ref[:, p, R - a : R - a + rows] + ref[:, p, R + a : R + a + rows])
     blocks = ref.shape[0]
     out = None
     for b in range(R):
@@ -80,10 +100,10 @@
         if b == 0:
             out = mid
             continue
-        lane = iota(mid.shape, 3)
+        lane = iota(mid.shape, 2)
         upper = jnp.where(lane < b, total[2:], mid)
         lower = jnp.where(lane >= LANES - b, total[: blocks - 2], mid)
-        out = out + pltpu.roll(upper, LANES - b, 3) + pltpu.roll(lower, b, 3)
+        out = out + pltpu.roll(upper, LANES - b, 2) + pltpu.roll(lower, b, 2)
     return out
 
 
@@ -300,13 +320,13 @@
 
     def shift_e(x):
         for z, n in CHUNKS:
-            EY[0, z : z + n] = ahead_y(E[0, x, z : z + n])
-            EY[1, z : z + n] = ahead_y(E[2, x, z : z + n])
+            own = slice(z, z + n)
+            EY[0, own], EY[1, own] = ahead_pair(E[0, x, own], E[2, x, own])
 
     def shift_h(x):
         for z, n in CHUNKS:
-            HY[0, z : z + n] = behind_y(H[0, x + 1, z + 1 : z + n + 1])
-            HY[1, z : z + n] = behind_y(H[2, x + 1, z + 1 : z + n + 1])
+            own, up = slice(z, z + n), slice(z + 1, z + n + 1)
+            HY[0, own], HY[1, own] = behind_pair(H[0, x + 1, up], H[2, x + 1, up])
 
     def layer_h(s, x):
         for z, n in CHUNKS:
@@ -477,7 +497,11 @@
     DF[:, :, R : R + X] = AG[around, DESIGN:SENS]
     for item in rows:
         pl.when(item[2])(item[0].wait_recv)
-    SL[...] = projection_slope(cone(DF, X))
+
+    @pl.loop(0, PLANES)
+    def _(p):
+        SL[:, p] = projection_slope(cone(DF, p, X))
+
     receive(1, copies)
 
     for p in range(PLANES):
@@ -541,9 +565,13 @@
 
     for item in edges:
         pl.when(item[2])(item[0].wait_recv)
-    result = cone(WV, X)
-    for block in range(TB):
-        gradient[:, :, block * LANES : (block + 1) * LANES] = result[block]
+
+    @pl.loop(0, PLANES)
+    def _(p):
+        result = cone(WV, p, X)
+        for block in range(TB):
+            gradient[p, :, block * LANES : (block + 1) * LANES] = result[block]
+
 
     for copy in gathers + partials:
         copy.wait_send()

time: 45.4 us -> 45.5 us (level)
  no operation moved by 1% of the time
where the time goes in v4:
time: 45.5 us; the launch traced here: 45.3 us
  Pallas kernels  38.6 us (85%)
  local copies, waits for them, and re-layouts  5.39 us (12%)
  between operations  1.29 us (3%)
    pallas_call x1, Pallas kernels, shards(): pl.pallas_call(functools.partial(kernel, gxn, gzn), out_shape=(pltpu.VMEM...  38.6 us
    unnamed x2, local copies, waits for them, and re-layouts  5.39 us

profile of v4, /device:TPU:1, one launch (start us, length us, event | category | flops | bytes accessed | tf_op | source)
XLA Modules:
  0.0 45.3 jit_solution(3210710809859078910)
XLA Ops:
  1.3 38.6 %shard_map.86 = (f32[6,16,32,8,128]{4,3,2,1,0:T(8,128)S(1)}, f32[2,16,256]{2,1,0:T(8,128)S(1)}) custom-call(f32[6,16,32,8,128]{4,3,2,1,0:T(8,128)} %fields.1, f32[16,32,8,128]{3,2,1,0:T(8,128)} %coef.1, s32[2]{0:T(128)} %plane_z.1, s32[1]{0:T(128)S(6)} %copy.13.snap_index, f32[4,2,3,16,256]{4,3,2,1,0:T(8,128)} %fwd_hbm.1, f32[2,16,256]{2,1,0:T(8,128)} %design_hbm.1, ...), custom_call_target="tpu_custom_call" | custom-call | tf_op jit(solution)/shard_map/pallas_call | solution.py:596
  39.9 4.8 %copy.11 = f32[6,16,32,8,128]{4,3,2,1,0:T(8,128)} copy(f32[6,16,32,8,128]{4,3,2,1,0:T(8,128)S(1)} %get-tuple-element.2) | data formatting | bytes 25165824
  44.7 0.6 %copy.12 = f32[2,16,256]{2,1,0:T(8,128)} copy(f32[2,16,256]{2,1,0:T(8,128)S(1)} %get-tuple-element.3) | data formatting | bytes 65536
